TPU v7x, 256 devices: a whole 4x4x8 slice. The times are simulated.
256 devices in a mesh: dp: 32 (over z, x_hi, core), tensor: 8 (over x_lo, y).
Axes of the slice: x: 4 (x_hi: 2, x_lo: 2; x = x_hi * 2 + x_lo), y: 4, z: 8, core: 2. Of those that a mesh axis runs over, the one named last changes fastest.
Arguments:
- picture_skip_entries: bfloat16 [8192, 1536], P('dp', 'tensor'), may hold values from -6 to 6
- picture_activations: bfloat16 [8192, 6144], P('dp', 'tensor'), may hold values from -6 to 6
- picture_contract_weights: bfloat16 [6144, 1536], P('tensor'), may hold values from -1 to 1
- picture_embedding_map: bfloat16 [1536, 1536], P('tensor'), may hold values from -1 to 1
- caption_skip_entries: bfloat16 [8192, 1536], P('dp', 'tensor'), may hold values from -6 to 6
- caption_activations: bfloat16 [8192, 6144], P('dp', 'tensor'), may hold values from -6 to 6
- caption_contract_weights: bfloat16 [6144, 1536], P('tensor'), may hold values from -1 to 1
- caption_embedding_map: bfloat16 [1536, 1536], P('tensor'), may hold values from -1 to 1
- sharpness_coefficient: float32 [1], replicated, may hold values from 5 to 12
- pairwise_score_shift: float32 [1], replicated, may hold values from -4 to -1
Outputs:
- grad_image_proj: float32 [1536, 1536], P('tensor', 'dp')
- grad_text_proj: float32 [1536, 1536], P('tensor', 'dp')
All inputs are finite; a program needn't handle non-finite values.
Results may differ from a plain program's by a relative error of at most 0.007.
Values may be sent and summed in bfloat16 or wider, within the bound.
A program may use at most 64 MiB of HBM per device.

v0:
```python
import jax
import jax.numpy as jnp
from jax import lax
from jax.sharding import PartitionSpec as P


def from_behind(block, axis, distance):
    devices = range(lax.axis_size(axis))
    route = [((i - distance) % len(devices), i) for i in devices]
    return lax.ppermute(block, axis, route)


def normalize(raw_embed):
    row_norm = jnp.sqrt(jnp.sum(raw_embed * raw_embed, axis=1, keepdims=True) + 1e-06)
    return (raw_embed / row_norm, row_norm)


def raw_gradient(grad_embed, unit_embed, row_norm):
    along_unit = jnp.sum(unit_embed * grad_embed, axis=1, keepdims=True)
    return ((grad_embed - unit_embed * along_unit) / row_norm).astype(jnp.bfloat16)


def pair_tile(
    text_rows, text_index, image_rows, image_start, pairwise_score_multiplier, logit_shift
):
    logits = (
        pairwise_score_multiplier
        * lax.dot_general(
            text_rows, image_rows, (((1,), (1,)), ((), ())), preferred_element_type=jnp.float32
        )
        + logit_shift
    )
    image_index = image_start + lax.broadcasted_iota(jnp.int32, (1, image_rows.shape[0]), 1)
    positive = text_index[:, None] == image_index
    return (
        pairwise_score_multiplier * (jax.nn.sigmoid(logits) - positive.astype(jnp.float32))
    ).astype(jnp.bfloat16)


def image_term(pair_coef, text_rows):
    return lax.dot_general(
        pair_coef, text_rows, (((0,), (0,)), ((), ())), preferred_element_type=jnp.float32
    )


def on_device(
    picture_skip_entries,
    picture_activations,
    picture_contract_weights,
    picture_embedding_map,
    caption_skip_entries,
    caption_activations,
    caption_contract_weights,
    caption_embedding_map,
    sharpness_coefficient,
    pairwise_score_shift,
):
    tensor_count = lax.axis_size("tensor")
    loop_count = lax.axis_size("dp")
    tensor_rank = lax.axis_index("tensor")
    loop_rank = lax.axis_index("dp")
    batch_dev = picture_skip_entries.shape[0]
    block_rows = batch_dev // tensor_count
    pairwise_score_multiplier = sharpness_coefficient[0]
    logit_shift = pairwise_score_shift[0]
    down_image = jnp.dot(
        picture_activations, picture_contract_weights, preferred_element_type=jnp.float32
    )
    down_text = jnp.dot(
        caption_activations, caption_contract_weights, preferred_element_type=jnp.float32
    )
    summed_image, summed_text = (
        lax.psum_scatter(
            down_image.astype(jnp.bfloat16), "tensor", scatter_dimension=1, tiled=True
        ).astype(jnp.float32),
        lax.psum_scatter(
            down_text.astype(jnp.bfloat16), "tensor", scatter_dimension=1, tiled=True
        ).astype(jnp.float32),
    )
    stream_image = (picture_skip_entries.astype(jnp.float32) + summed_image).astype(jnp.bfloat16)
    stream_text = (caption_skip_entries.astype(jnp.float32) + summed_text).astype(jnp.bfloat16)
    partial_image = jnp.dot(stream_image, picture_embedding_map, preferred_element_type=jnp.float32)
    partial_text = jnp.dot(stream_text, caption_embedding_map, preferred_element_type=jnp.float32)
    raw_image, raw_text = (
        lax.psum_scatter(
            partial_image.astype(jnp.bfloat16), "tensor", scatter_dimension=0, tiled=True
        ).astype(jnp.float32),
        lax.psum_scatter(
            partial_text.astype(jnp.bfloat16), "tensor", scatter_dimension=0, tiled=True
        ).astype(jnp.float32),
    )
    unit_image, norm_image = normalize(raw_image)
    image_rows = lax.all_gather(unit_image.astype(jnp.bfloat16), "tensor", axis=0, tiled=True)
    unit_text, norm_text = normalize(raw_text)
    text_rows = unit_text.astype(jnp.bfloat16)
    image_start = loop_rank * batch_dev
    text_offset = tensor_rank * block_rows
    width = text_rows.shape[1]
    zero_image = jnp.zeros((batch_dev, width), jnp.float32)
    block_iota = lax.iota(jnp.int32, block_rows)

    def advance(turn_index, carried):
        moving_rows, moving_sum, image_grad = carried
        anchor = (loop_rank - turn_index) % loop_count
        text_index = anchor * batch_dev + text_offset + block_iota
        pair_coef = pair_tile(
            moving_rows, text_index, image_rows, image_start, pairwise_score_multiplier, logit_shift
        )
        image_grad = image_grad + image_term(pair_coef, moving_rows)
        moving_sum = moving_sum + jnp.dot(pair_coef, image_rows, preferred_element_type=jnp.float32)
        moving_rows = from_behind(moving_rows, "dp", 1)
        moving_sum = from_behind(moving_sum, "dp", 1)
        return (moving_rows, moving_sum, image_grad)

    start_carry = (text_rows, jnp.zeros((block_rows, width), jnp.float32), zero_image)
    final_carry = lax.fori_loop(0, loop_count, advance, start_carry)
    text_grad = final_carry[1]
    image_grad = final_carry[2]
    image_total = lax.psum_scatter(image_grad, "tensor", scatter_dimension=0, tiled=True)
    image_raw, text_raw = (
        lax.all_gather(
            raw_gradient(image_total, unit_image, norm_image), "tensor", axis=0, tiled=True
        ),
        lax.all_gather(raw_gradient(text_grad, unit_text, norm_text), "tensor", axis=0, tiled=True),
    )
    term_image = lax.dot_general(
        stream_image, image_raw, (((0,), (0,)), ((), ())), preferred_element_type=jnp.float32
    )
    term_text = lax.dot_general(
        stream_text, text_raw, (((0,), (0,)), ((), ())), preferred_element_type=jnp.float32
    )
    grad_image_proj, grad_text_proj = (
        lax.psum_scatter(term_image, "dp", scatter_dimension=1, tiled=True),
        lax.psum_scatter(term_text, "dp", scatter_dimension=1, tiled=True),
    )
    return (grad_image_proj, grad_text_proj)


def solution(mesh):
    placed = (
        P("dp", "tensor"),
        P("dp", "tensor"),
        P("tensor", None),
        P("tensor", None),
        P("dp", "tensor"),
        P("dp", "tensor"),
        P("tensor", None),
        P("tensor", None),
        P(),
        P(),
    )
    return jax.shard_map(
        on_device,
        mesh=mesh,
        in_specs=placed,
        out_specs=(P("tensor", "dp"), P("tensor", "dp")),
        check_vma=False,
    )
```

profile of v0, /device:TPU:1, one launch (start us, length us, event | category | flops | bytes accessed | tf_op | source)
XLA Modules:
  0.0 842.8 jit_solution(12933953244024127879)
XLA Ops:
  11.9 3.6 convolution_convert_fusion
  15.6 35.9 %reduce-scatter.8.cloned.1.call-done = bf16[256,192]{0,1:T(8,128)(2,1)} async-done(((bf16[256,1536]{0,1:T(8,128)(2,1)}), bf16[256,192]{0,1:T(8,128)(2,1)}) %reduce-scatter.8.cloned.1.call-update) | async-done | bytes 98320 | tf_op jit(solution)/shard_map/reduce_scatter | solution.py:73
  53.8 40.1 %reduce-scatter.10.cloned.1.call-done = bf16[256,192]{0,1:T(8,128)(2,1)} async-done(((bf16[256,1536]{0,1:T(8,128)(2,1)}), bf16[256,192]{0,1:T(8,128)(2,1)}) %reduce-scatter.10.cloned.1.call-update) | async-done | bytes 98320 | tf_op jit(solution)/shard_map/reduce_scatter | solution.py:76
  96.2 39.9 %reduce-scatter.14.cloned.1.call-done = bf16[32,1536]{1,0:T(8,128)(2,1)} async-done(((bf16[256,1536]{1,0:T(8,128)(2,1)}), bf16[32,1536]{1,0:T(8,128)(2,1)}) %reduce-scatter.14.cloned.1.call-update) | async-done | bytes 98320 | tf_op jit(solution)/shard_map/reduce_scatter | solution.py:85
  138.8 23.8 %all_gather.9 = bf16[256,1536]{1,0:T(8,128)(2,1)S(1)} all-gather(bf16[32,1536]{1,0:T(8,128)(2,1)S(1)} %fusion.15), channel_id=1, replica_groups=mesh['dp'=32,'tensor'=8] {'tensor'}, dimensions={0}, use_global_device_ids=true | all-gather | bytes 884736 | tf_op jit(solution)/shard_map/all_gather | solution.py:93
  162.6 17.5 %reduce-scatter.12.cloned.1.call-done = bf16[32,1536]{1,0:T(8,128)(2,1)} async-done(((bf16[256,1536]{1,0:T(8,128)(2,1)}), bf16[32,1536]{1,0:T(8,128)(2,1)}) %reduce-scatter.12.cloned.1.call-update) | async-done | bytes 98320 | tf_op jit(solution)/shard_map/reduce_scatter | solution.py:88
  182.2 369.9 %while.20 = (s32[]{:T(128)}, bf16[32,1536]{1,0:T(8,128)(2,1)S(1)}, f32[32,1536]{1,0:T(8,128)S(1)}, f32[256,1536]{1,0:T(8,128)}, f32[]{:T(128)}, /*index=5*/bf16[...) while((s32[]{:T(128)}, bf16[32,1536]{1,0:T(8,128)(2,1)S(1)}, ...), condition=%wide.region_7.8_spmd.clone, body=%wide.region_6.7_spmd.clone.sunk | while | flops 76415280 | bytes 6736520 | solution.py:116
  182.2 7.2 collective-permute-start
  195.0 4.0 collective-permute-start
  204.5 3.9 collective-permute-start
  214.2 3.8 collective-permute-start
  257.8 3.0 collective-permute-done.1
  269.4 3.0 collective-permute-done.1
  316.0 3.0 collective-permute-done.1
  327.6 3.0 collective-permute-done.1
  374.2 3.0 collective-permute-done.1
  432.5 3.0 collective-permute-done.1
  490.7 3.0 collective-permute-done.1
  546.0 3.1 collective-permute-done
  553.3 25.3 %all_gather.11 = bf16[256,1536]{1,0:T(8,128)(2,1)S(1)} all-gather(bf16[32,1536]{1,0:T(8,128)(2,1)S(1)} %divide_convert_fusion), channel_id=1, replica_groups=mesh['dp'=32,'tensor'=8] {'tensor'}, dimensions={0}, use_global_device_ids=true | all-gather | bytes 884736 | tf_op jit(solution)/shard_map/all_gather | solution.py:124
  580.3 16.2 %reduce-scatter.16.cloned.1.call-done = f32[32,1536]{1,0:T(8,128)} async-done(((f32[256,1536]{1,0:T(8,128)}), f32[32,1536]{1,0:T(8,128)}) %reduce-scatter.16.cloned.1.call-update) | async-done | bytes 196624 | tf_op jit(solution)/shard_map/reduce_scatter | solution.py:119
  598.7 23.6 %all_gather.10 = bf16[256,1536]{1,0:T(8,128)(2,1)S(1)} all-gather(bf16[32,1536]{1,0:T(8,128)(2,1)S(1)} %divide_convert_fusion.1), channel_id=1, replica_groups=mesh['dp'=32,'tensor'=8] {'tensor'}, dimensions={0}, use_global_device_ids=true | all-gather | bytes 884736 | tf_op jit(solution)/shard_map/all_gather | solution.py:121
  623.9 91.9 %reduce-scatter.20.cloned.1.call-done = f32[192,48]{0,1:T(8,128)} async-done(((f32[192,1536]{0,1:T(8,128)}), f32[192,48]{0,1:T(8,128)}) %reduce-scatter.20.cloned.1.call-update) | async-done | bytes 36880 | tf_op jit(solution)/shard_map/reduce_scatter | solution.py:134
  715.8 120.1 %reduce-scatter.18.cloned.1.call-done = f32[192,48]{0,1:T(8,128)} async-done(((f32[192,1536]{0,1:T(8,128)}), f32[192,48]{0,1:T(8,128)}) %reduce-scatter.18.cloned.1.call-update) | async-done | bytes 36880 | tf_op jit(solution)/shard_map/reduce_scatter | solution.py:133
  (367 shorter events, 345.9 us)
Async XLA Ops:
  7.2 44.3 %reduce-scatter.8.cloned.1.call-start = ((), (), s32[]{:S(2)}) async-start(), calls=%async_computation.7 | async-start | bytes 884736 | tf_op jit(solution)/shard_map/reduce_scatter | solution.py:73
  11.8 82.1 %reduce-scatter.10.cloned.1.call-start = ((), (), s32[]{:S(2)}) async-start(), calls=%async_computation.8 | async-start | bytes 884736 | tf_op jit(solution)/shard_map/reduce_scatter | solution.py:76
  15.5 120.6 %reduce-scatter.14.cloned.1.call-start = ((), (), s32[]{:S(2)}) async-start(), calls=%async_computation.10 | async-start | bytes 884736 | tf_op jit(solution)/shard_map/reduce_scatter | solution.py:85
  53.8 126.4 %reduce-scatter.12.cloned.1.call-start = ((), (), s32[]{:S(2)}) async-start(), calls=%async_computation.9 | async-start | bytes 884736 | tf_op jit(solution)/shard_map/reduce_scatter | solution.py:88
  96.1 500.4 %reduce-scatter.16.cloned.1.call-start = ((), (), s32[]{:S(2)}) async-start(), calls=%async_computation.11 | async-start | bytes 1769472 | tf_op jit(solution)/shard_map/reduce_scatter | solution.py:119
  182.2 11.4 %collective-permute-start = (bf16[32,1536]{1,0:T(8,128)(2,1)S(1)}, bf16[32,1536]{1,0:T(8,128)(2,1)S(1)}, u32[]{:S(2)}, u32[]{:S(2)}) collective-permute-start(bf16[32,1536]{1,0:T(8,128)(2,1)S(1)} %copy.17), channel_id=1, source_target_pairs={{248,0},{0,8},{8,16},{16,24},{24,32},{32,40},{40,48},{48,56},{56,6... | collective-permute-start | bytes 294920 | tf_op jit(solution)/shard_map/while/body/eval_jaxpr/ppermute | solution.py:10
  195.0 9.6 %collective-permute-start = (bf16[32,1536]{1,0:T(8,128)(2,1)S(1)}, bf16[32,1536]{1,0:T(8,128)(2,1)S(1)}, u32[]{:S(2)}, u32[]{:S(2)}) collective-permute-start(bf16[32,1536]{1,0:T(8,128)(2,1)S(1)} %copy.17), channel_id=1, source_target_pairs={{248,0},{0,8},{8,16},{16,24},{24,32},{32,40},{40,48},{48,56},{56,6... | collective-permute-start | bytes 294920 | tf_op jit(solution)/shard_map/while/body/eval_jaxpr/ppermute | solution.py:10
  204.5 9.5 %collective-permute-start = (bf16[32,1536]{1,0:T(8,128)(2,1)S(1)}, bf16[32,1536]{1,0:T(8,128)(2,1)S(1)}, u32[]{:S(2)}, u32[]{:S(2)}) collective-permute-start(bf16[32,1536]{1,0:T(8,128)(2,1)S(1)} %copy.17), channel_id=1, source_target_pairs={{248,0},{0,8},{8,16},{16,24},{24,32},{32,40},{40,48},{48,56},{56,6... | collective-permute-start | bytes 294920 | tf_op jit(solution)/shard_map/while/body/eval_jaxpr/ppermute | solution.py:10
  214.2 9.4 %collective-permute-start = (bf16[32,1536]{1,0:T(8,128)(2,1)S(1)}, bf16[32,1536]{1,0:T(8,128)(2,1)S(1)}, u32[]{:S(2)}, u32[]{:S(2)}) collective-permute-start(bf16[32,1536]{1,0:T(8,128)(2,1)S(1)} %copy.17), channel_id=1, source_target_pairs={{248,0},{0,8},{8,16},{16,24},{24,32},{32,40},{40,48},{48,56},{56,6... | collective-permute-start | bytes 294920 | tf_op jit(solution)/shard_map/while/body/eval_jaxpr/ppermute | solution.py:10
  251.8 8.9 %collective-permute-start.1 = (f32[32,1536]{1,0:T(8,128)}, f32[32,1536]{1,0:T(8,128)S(1)}, u32[]{:S(2)}, u32[]{:S(2)}) collective-permute-start(f32[32,1536]{1,0:T(8,128)} %convolution_add_fusion.4), channel_id=1, source_target_pairs={{248,0},{0,8},{8,16},{16,24},{24,32},{32,40},{40,48},{48,56},{56,6... | collective-permute-start | bytes 589832 | tf_op jit(solution)/shard_map/while/body/eval_jaxpr/ppermute | solution.py:10
  263.5 8.9 %collective-permute-start.1 = (f32[32,1536]{1,0:T(8,128)}, f32[32,1536]{1,0:T(8,128)S(1)}, u32[]{:S(2)}, u32[]{:S(2)}) collective-permute-start(f32[32,1536]{1,0:T(8,128)} %convolution_add_fusion.4), channel_id=1, source_target_pairs={{248,0},{0,8},{8,16},{16,24},{24,32},{32,40},{40,48},{48,56},{56,6... | collective-permute-start | bytes 589832 | tf_op jit(solution)/shard_map/while/body/eval_jaxpr/ppermute | solution.py:10
  298.4 8.9 %collective-permute-start.1 = (f32[32,1536]{1,0:T(8,128)}, f32[32,1536]{1,0:T(8,128)S(1)}, u32[]{:S(2)}, u32[]{:S(2)}) collective-permute-start(f32[32,1536]{1,0:T(8,128)} %convolution_add_fusion.4), channel_id=1, source_target_pairs={{248,0},{0,8},{8,16},{16,24},{24,32},{32,40},{40,48},{48,56},{56,6... | collective-permute-start | bytes 589832 | tf_op jit(solution)/shard_map/while/body/eval_jaxpr/ppermute | solution.py:10
  310.1 8.9 %collective-permute-start.1 = (f32[32,1536]{1,0:T(8,128)}, f32[32,1536]{1,0:T(8,128)S(1)}, u32[]{:S(2)}, u32[]{:S(2)}) collective-permute-start(f32[32,1536]{1,0:T(8,128)} %convolution_add_fusion.4), channel_id=1, source_target_pairs={{248,0},{0,8},{8,16},{16,24},{24,32},{32,40},{40,48},{48,56},{56,6... | collective-permute-start | bytes 589832 | tf_op jit(solution)/shard_map/while/body/eval_jaxpr/ppermute | solution.py:10
  321.7 8.9 %collective-permute-start.1 = (f32[32,1536]{1,0:T(8,128)}, f32[32,1536]{1,0:T(8,128)S(1)}, u32[]{:S(2)}, u32[]{:S(2)}) collective-permute-start(f32[32,1536]{1,0:T(8,128)} %convolution_add_fusion.4), channel_id=1, source_target_pairs={{248,0},{0,8},{8,16},{16,24},{24,32},{32,40},{40,48},{48,56},{56,6... | collective-permute-start | bytes 589832 | tf_op jit(solution)/shard_map/while/body/eval_jaxpr/ppermute | solution.py:10
  356.7 8.9 %collective-permute-start.1 = (f32[32,1536]{1,0:T(8,128)}, f32[32,1536]{1,0:T(8,128)S(1)}, u32[]{:S(2)}, u32[]{:S(2)}) collective-permute-start(f32[32,1536]{1,0:T(8,128)} %convolution_add_fusion.4), channel_id=1, source_target_pairs={{248,0},{0,8},{8,16},{16,24},{24,32},{32,40},{40,48},{48,56},{56,6... | collective-permute-start | bytes 589832 | tf_op jit(solution)/shard_map/while/body/eval_jaxpr/ppermute | solution.py:10
  368.3 8.9 %collective-permute-start.1 = (f32[32,1536]{1,0:T(8,128)}, f32[32,1536]{1,0:T(8,128)S(1)}, u32[]{:S(2)}, u32[]{:S(2)}) collective-permute-start(f32[32,1536]{1,0:T(8,128)} %convolution_add_fusion.4), channel_id=1, source_target_pairs={{248,0},{0,8},{8,16},{16,24},{24,32},{32,40},{40,48},{48,56},{56,6... | collective-permute-start | bytes 589832 | tf_op jit(solution)/shard_map/while/body/eval_jaxpr/ppermute | solution.py:10
  379.9 8.9 %collective-permute-start.1 = (f32[32,1536]{1,0:T(8,128)}, f32[32,1536]{1,0:T(8,128)S(1)}, u32[]{:S(2)}, u32[]{:S(2)}) collective-permute-start(f32[32,1536]{1,0:T(8,128)} %convolution_add_fusion.4), channel_id=1, source_target_pairs={{248,0},{0,8},{8,16},{16,24},{24,32},{32,40},{40,48},{48,56},{56,6... | collective-permute-start | bytes 589832 | tf_op jit(solution)/shard_map/while/body/eval_jaxpr/ppermute | solution.py:10
  414.9 8.9 %collective-permute-start.1 = (f32[32,1536]{1,0:T(8,128)}, f32[32,1536]{1,0:T(8,128)S(1)}, u32[]{:S(2)}, u32[]{:S(2)}) collective-permute-start(f32[32,1536]{1,0:T(8,128)} %convolution_add_fusion.4), channel_id=1, source_target_pairs={{248,0},{0,8},{8,16},{16,24},{24,32},{32,40},{40,48},{48,56},{56,6... | collective-permute-start | bytes 589832 | tf_op jit(solution)/shard_map/while/body/eval_jaxpr/ppermute | solution.py:10
  426.5 8.9 %collective-permute-start.1 = (f32[32,1536]{1,0:T(8,128)}, f32[32,1536]{1,0:T(8,128)S(1)}, u32[]{:S(2)}, u32[]{:S(2)}) collective-permute-start(f32[32,1536]{1,0:T(8,128)} %convolution_add_fusion.4), channel_id=1, source_target_pairs={{248,0},{0,8},{8,16},{16,24},{24,32},{32,40},{40,48},{48,56},{56,6... | collective-permute-start | bytes 589832 | tf_op jit(solution)/shard_map/while/body/eval_jaxpr/ppermute | solution.py:10
  438.2 8.9 %collective-permute-start.1 = (f32[32,1536]{1,0:T(8,128)}, f32[32,1536]{1,0:T(8,128)S(1)}, u32[]{:S(2)}, u32[]{:S(2)}) collective-permute-start(f32[32,1536]{1,0:T(8,128)} %convolution_add_fusion.4), channel_id=1, source_target_pairs={{248,0},{0,8},{8,16},{16,24},{24,32},{32,40},{40,48},{48,56},{56,6... | collective-permute-start | bytes 589832 | tf_op jit(solution)/shard_map/while/body/eval_jaxpr/ppermute | solution.py:10
  484.8 8.9 %collective-permute-start.1 = (f32[32,1536]{1,0:T(8,128)}, f32[32,1536]{1,0:T(8,128)S(1)}, u32[]{:S(2)}, u32[]{:S(2)}) collective-permute-start(f32[32,1536]{1,0:T(8,128)} %convolution_add_fusion.4), channel_id=1, source_target_pairs={{248,0},{0,8},{8,16},{16,24},{24,32},{32,40},{40,48},{48,56},{56,6... | collective-permute-start | bytes 589832 | tf_op jit(solution)/shard_map/while/body/eval_jaxpr/ppermute | solution.py:10
  543.0 9.0 %collective-permute-start.1 = (f32[32,1536]{1,0:T(8,128)}, f32[32,1536]{1,0:T(8,128)S(1)}, u32[]{:S(2)}, u32[]{:S(2)}) collective-permute-start(f32[32,1536]{1,0:T(8,128)} %convolution_add_fusion.4), channel_id=1, source_target_pairs={{248,0},{0,8},{8,16},{16,24},{24,32},{32,40},{40,48},{48,56},{56,6... | collective-permute-start | bytes 589832 | tf_op jit(solution)/shard_map/while/body/eval_jaxpr/ppermute | solution.py:10
  552.1 163.8 %reduce-scatter.20.cloned.1.call-start = ((), (), s32[]{:S(2)}) async-start(), calls=%async_computation.13 | async-start | bytes 1622016 | tf_op jit(solution)/shard_map/reduce_scatter | solution.py:134
  580.2 255.7 %reduce-scatter.18.cloned.1.call-start = ((), (), s32[]{:S(2)}) async-start(), calls=%async_computation.12 | async-start | bytes 1622016 | tf_op jit(solution)/shard_map/reduce_scatter | solution.py:133
  (61 other events, 687.8 us)
Sparse Core Ops, SparseCore 0:
  11.9 39.5 reduce-scatter.7
  54.2 39.6 reduce-scatter.9
  96.4 39.6 reduce-scatter.13
  138.7 41.3 reduce-scatter.11
  552.2 44.2 reduce-scatter.15
  601.0 114.7 reduce-scatter.19
  720.5 115.3 reduce-scatter.17
where the time goes:
time: 849 us; the launch traced here: 843 us
  waiting for transfers between devices  529 us (62%)
  matrix products  190 us (22%)
  blocking collectives  72.8 us (9%)
  starting transfers between devices  25.5 us (3%)
  between operations  14.3 us (2%)
    ppermute x64, waiting for transfers between devices, from_behind(): return lax.ppermute(block, axis, route)  167 us
    reduce_scatter x1, waiting for transfers between devices, on_device(): lax.psum_scatter(term_image, 'dp', scatter_dimension=1, tiled=True)  120 us
    dot_general x32, matrix products, image_term(): lax.dot_general(pair_coef, text_rows, (((0,), (0,)), ((), ())), preferred...  93.1 us
    reduce_scatter x1, waiting for transfers between devices, on_device(): lax.psum_scatter(term_text, 'dp', scatter_dimension=1, tiled=True)  91.9 us
    dot_general x32, matrix products, pair_tile(): lax.dot_general(text_rows, image_rows, (((1,), (1,)), ((), ())), preferre...  52.6 us
    reduce_scatter x1, waiting for transfers between devices, on_device(): lax.psum_scatter(down_text.astype(jnp.bfloat16), 'tensor', scatter_dimens...  40.1 us
    reduce_scatter x1, waiting for transfers between devices, on_device(): lax.psum_scatter(partial_image.astype(jnp.bfloat16), 'tensor', scatter_di...  39.9 us
    reduce_scatter x1, waiting for transfers between devices, on_device(): lax.psum_scatter(down_image.astype(jnp.bfloat16), 'tensor', scatter_dimen...  35.9 us
  transfers between devices with their start and end apart: 71, of which 66 were waited for; matrix products, arithmetic and copies ran while one was open for 23% of the time, Pallas kernels for 0%

commit v1 on v0

v1 whole, which is shorter than its diff:
```python
from types import SimpleNamespace

import jax
import jax.numpy as jnp
from jax import lax
from jax.experimental import pallas as pl
from jax.experimental.pallas import tpu as pltpu
from jax.sharding import PartitionSpec as P

MESH = pl.DeviceIdType.MESH
BF16, F32 = jnp.bfloat16, jnp.float32
VMEM_LIMIT = 60 * 1024 * 1024


def device(z, x, y, c):
    return (z * 4 + x // 2 * 2 + c, x % 2 * 4 + y)


def push(src, dst, send, recv, peer):
    copy = pltpu.make_async_remote_copy(
        src_ref=src, dst_ref=dst, send_sem=send, recv_sem=recv, device_id=peer, device_id_type=MESH
    )
    copy.start()
    return copy


def raw_gradient(grad, unit, norm):
    along = jnp.sum(unit * grad, axis=1, keepdims=True)
    return ((grad - unit * along) / norm).astype(BF16)


def scatter_scratch(one, other):
    return dict(
        one=pltpu.VMEM((2, 8, *one), BF16),
        other=pltpu.VMEM((2, 8, *other), BF16),
        cross_in=pltpu.VMEM((2, 4, *one), BF16),
        half_out=pltpu.VMEM((2, 4, *one), BF16),
        half_in=pltpu.VMEM((2, 4, *one), BF16),
        round_out=pltpu.VMEM((2, 2, *other), BF16),
        round_in=pltpu.VMEM((2, 6, *other), BF16),
        wide_out=pltpu.VMEM((2, 2, *other), BF16),
        wide_in=pltpu.VMEM((2, *other), BF16),
        sem=pltpu.SemaphoreType.DMA((2, 2, 12)),
    )


DOWN = scatter_scratch((80, 256), (112, 256))
EMB = scatter_scratch((32, 640), (32, 896))
SCRATCH = dict(
    act=pltpu.VMEM((2, 256, 768), BF16),
    w=pltpu.VMEM((2, 768, 1536), BF16),
    m=pltpu.VMEM((2, 192, 1536), BF16),
    skip=pltpu.VMEM((2, 192, 256), BF16),
    stream=pltpu.VMEM((8, 2, 192, 256), BF16),
    unit=pltpu.VMEM((2, 32, 1536), F32),
    norm=pltpu.VMEM((2, 32, 128), F32),
    img=pltpu.VMEM((2, 4, 4, 16, 1536), BF16),
    txt=pltpu.VMEM((2, 8, 32, 1536), BF16),
    coef=pltpu.VMEM((2, 256, 512), BF16),
    coef_t=pltpu.VMEM((2, 256, 512), BF16),
    gt_own=pltpu.VMEM((8, 32, 1536), F32),
    gt_out=pltpu.VMEM((8, 32, 1536), BF16),
    gt_in=pltpu.VMEM((8, 32, 1536), BF16),
    gz_out=pltpu.VMEM((8, 32, 1536), BF16),
    gz_in=pltpu.VMEM((8, 32, 1536), BF16),
    gi_out=pltpu.VMEM((2, 4, 4, 16, 1536), BF16),
    gi_in=pltpu.VMEM((2, 4, 4, 16, 1536), BF16),
    gh_out=pltpu.VMEM((2, 4, 16, 1536), BF16),
    gh_in=pltpu.VMEM((2, 4, 16, 1536), BF16),
    pack=pltpu.VMEM((2, 8, 16, 384), BF16),
    graw=pltpu.VMEM((2, 8, 8, 16, 384), BF16),
    part=pltpu.VMEM((2, 2, 48, 384), F32),
    part_in=pltpu.VMEM((2, 48, 384), F32),
    last_out=pltpu.VMEM((48, 384), F32),
    last_in=pltpu.VMEM((48, 384), F32),
    load_sem=pltpu.SemaphoreType.DMA((2, 7)),
    stream_sem=pltpu.SemaphoreType.DMA((2, 9)),
    img_sem=pltpu.SemaphoreType.DMA((2, 3, 2, 4)),
    txt_sem=pltpu.SemaphoreType.DMA((2, 8, 2)),
    pair_sem=pltpu.SemaphoreType.DMA((2, 8)),
    gt_sem=pltpu.SemaphoreType.DMA((2,)),
    gz_sem=pltpu.SemaphoreType.DMA((2, 8, 2)),
    gi_sem=pltpu.SemaphoreType.DMA((2, 3, 2, 4)),
    turn_sem=pltpu.SemaphoreType.DMA((2, 2, 8)),
    spread_sem=pltpu.SemaphoreType.DMA((2, 2, 3, 8)),
    part_sem=pltpu.SemaphoreType.DMA((2, 2)),
)


def window_kernel(*refs):
    inputs, (scale_ref, shift_ref), output = refs[:8], refs[8:10], refs[10]
    count = len(SCRATCH)
    v = SimpleNamespace(**dict(zip(SCRATCH, refs[11:])))
    v.down = SimpleNamespace(**dict(zip(DOWN, refs[11 + count :])))
    v.emb = SimpleNamespace(**dict(zip(EMB, refs[11 + count + len(DOWN) :])))
    for s in (v.down, v.emb):
        s.relay, s.cross, s.near, s.last, s.along, s.wide = ({} for _ in range(6))
    d, t = lax.axis_index("dp"), lax.axis_index("tensor")
    z, x, y, c = d // 4, d // 2 % 2 * 2 + t // 4, t % 4, d % 2
    sends = []

    def send(*args):
        copy = push(*args)
        sends.append(copy)
        return copy

    def to_x(k):
        return device(z, (x + k) % 4, y, c)

    def to_y(k):
        return (d, t // 4 * 4 + (y + k) % 4)

    def to_z(k):
        return ((z + k) % 8 * 4 + d % 4, t)

    sibling = (d // 2 * 2 + 1 - c, t)

    loads = {}
    for tower in (1, 0):
        act, w, m, skip = inputs[tower * 4 : tower * 4 + 4]
        pairs = [(act, v.act.at[tower])]
        for f in range(4):
            cols = pl.ds(f * 384, 384)
            pairs.append((w.at[:, cols], v.w.at[tower, :, cols]))
        pairs += [(m, v.m.at[tower]), (skip, v.skip.at[tower])]
        row = []
        for j, (source, target) in enumerate(pairs):
            load = pltpu.make_async_copy(source, target, v.load_sem.at[tower, j])
            load.start()
            row.append(load)
        loads[tower] = row

    peers = [(d, (t + k) % 8) for k in range(1, 8)]
    peers += [to_z(k) for k in range(1, 8)]
    peers += [device(z, (x + 2) % 4, y, c), device(z, (x // 2 * 2 + 2) % 4 + 1 - x % 2, y, c)]
    peers += [sibling]
    barrier = pltpu.get_barrier_semaphore()
    for peer in peers:
        pl.semaphore_signal(barrier, inc=1, device_id=peer, device_id_type=MESH)

    low = t // 4
    partner = (d, (t + 4) % 8)

    def scatter_start(s, tower):
        def hop(j, k, wide, way):
            return send(
                s.other.at[tower, wide * 4 + (y + k) % 4],
                s.round_in.at[tower, j],
                s.sem.at[0, tower, j],
                s.sem.at[1, tower, j],
                to_y(way),
            )

        s.relay[tower] = [hop(0, 2, 0, 1), hop(1, 2, 1, -1)]
        s.cross[tower] = send(
            s.one.at[tower, pl.ds((1 - low) * 4, 4)],
            s.cross_in.at[tower],
            s.sem.at[0, tower, 6],
            s.sem.at[1, tower, 6],
            partner,
        )
        s.near[tower] = [hop(2, 1, 1, 1), hop(3, 3, 0, -1)]

    def half_sum(s, tower, k):
        place = (y + k) % 4
        return s.one[tower, low * 4 + place].astype(F32) + s.cross_in[tower, place].astype(F32)

    def scatter_relay(s, tower):
        s.last[tower] = []
        for j, way in ((0, 1), (1, -1)):
            s.relay[tower][j].wait_recv()
            total = s.other[tower, j * 4 + (y + way) % 4].astype(F32)
            total += s.round_in[tower, j].astype(F32)
            s.round_out[tower, j] = total.astype(BF16)
            s.last[tower].append(
                send(
                    s.round_out.at[tower, j],
                    s.round_in.at[tower, 4 + j],
                    s.sem.at[0, tower, 4 + j],
                    s.sem.at[1, tower, 4 + j],
                    to_y(way),
                )
            )

    def scatter_along(s, tower):
        s.cross[tower].wait_recv()
        s.along[tower] = []
        for k in (2, 1, 3):
            s.half_out[tower, k] = half_sum(s, tower, k).astype(BF16)
            s.along[tower].append(
                send(
                    s.half_out.at[tower, k],
                    s.half_in.at[tower, k],
                    s.sem.at[0, tower, 7 + k],
                    s.sem.at[1, tower, 7 + k],
                    to_y(k),
                )
            )

    def scatter_wide(s, tower):
        for j in range(2):
            s.near[tower][1 - j].wait_recv()
            s.last[tower][j].wait_recv()
            total = s.other[tower, j * 4 + y].astype(F32)
            total += s.round_in[tower, 3 - j].astype(F32)
            total += s.round_in[tower, 4 + j].astype(F32)
            s.wide_out[tower, j] = total.astype(BF16)
        s.wide[tower] = send(
            s.wide_out.at[tower, 1 - low],
            s.wide_in.at[tower],
            s.sem.at[0, tower, 11],
            s.sem.at[1, tower, 11],
            partner,
        )

    def scatter_end(s, tower, axis):
        first = half_sum(s, tower, 0)
        for k in (1, 3, 2):
            s.along[tower][(2, 1, 3).index(k)].wait_recv()
            first += s.half_in[tower, k].astype(F32)
        s.wide[tower].wait_recv()
        second = s.wide_out[tower, low].astype(F32) + s.wide_in[tower].astype(F32)
        return jnp.concatenate([first, second], axis=axis)

    def down_projection(tower):
        loads[tower][0].wait()
        for f in range(4):
            loads[tower][1 + f].wait()
            product = jnp.dot(
                v.act[tower], v.w[tower, :, f * 384 : f * 384 + 384], preferred_element_type=F32
            )
            product = product.T.reshape(2, 192, 256).astype(BF16)
            v.down.one[tower, 2 * f : 2 * f + 2] = product[:, :80]
            v.down.other[tower, 2 * f : 2 * f + 2] = product[:, 80:]

        if tower == 1:
            pl.semaphore_wait(barrier, len(peers))
        scatter_start(v.down, tower)

    source = lax.broadcasted_iota(jnp.int32, (256, 256), 0)
    target = lax.broadcasted_iota(jnp.int32, (256, 256), 1)
    wanted = (target & 112) * 2 + (target & 15) + lax.shift_right_logical(target & 128, 3)
    reorder = (source == wanted).astype(F32).astype(BF16)

    def embedding_projection(tower):
        loads[tower][5].wait()
        loads[tower][6].wait()
        total = v.skip[tower].astype(F32) + scatter_end(v.down, tower, 0)
        columns = total.astype(BF16)
        rows = columns.T

        for f in range(6):
            product = jnp.dot(
                rows, v.m[tower, :, f * 256 : f * 256 + 256], preferred_element_type=F32
            )
            product = product.reshape(8, 32, 256).astype(BF16)
            cut = min(max(640 - f * 256, 0), 256)
            if cut > 0:
                v.emb.one[tower, :, :, f * 256 : f * 256 + cut] = product[:, :, :cut]
            if cut < 256:
                start = f * 256 + cut - 640
                v.emb.other[tower, :, :, start : start + 256 - cut] = product[:, :, cut:]

        scatter_start(v.emb, tower)
        v.stream[0, tower] = jnp.dot(columns, reorder, preferred_element_type=F32).astype(BF16)

    def await_all(copies):
        for copy in copies:
            copy.wait_recv()

    def stream_step(step):
        if step < 4:
            ways = ((1, (step - 1,), (step,), step), (-1, ((9 - step) % 8,), (8 - step,), 8 - step))
        else:
            ways = ((1, (3, 0), (4, 0), 4), (-1, (5, 1), (4, 1), 8))
        return [
            send(
                v.stream.at[at], v.stream.at[to], v.stream_sem.at[0, j], v.stream_sem.at[1, j], to_z(way)
            )
            for way, at, to, j in ways
        ]

    first, second = 1, 0
    down_projection(first)
    down_projection(second)
    scatter_relay(v.down, first)
    scatter_along(v.down, first)
    scatter_relay(v.down, second)
    scatter_wide(v.down, first)
    scatter_along(v.down, second)
    scatter_wide(v.down, second)
    embedding_projection(first)
    embedding_projection(second)
    stream_ring = stream_step(1)
    scatter_relay(v.emb, first)
    scatter_along(v.emb, first)
    scatter_relay(v.emb, second)
    scatter_wide(v.emb, first)
    scatter_along(v.emb, second)
    scatter_wide(v.emb, second)
    await_all(stream_ring)
    stream_ring = stream_step(2)

    def embed(tower):
        raw = scatter_end(v.emb, tower, 1)
        norm = jnp.sqrt(jnp.sum(raw * raw, axis=1, keepdims=True) + 1e-06)
        unit = raw / norm
        v.unit[tower] = unit
        v.norm[tower] = jnp.broadcast_to(norm, (32, 128))
        return unit.astype(BF16)

    v.txt[0, 0] = embed(1)
    pair_copies = []
    txt_copies = {}

    def share(slot):
        pair_copies.append(
            send(v.txt.at[0, slot], v.txt.at[1, slot], v.pair_sem.at[0, slot], v.pair_sem.at[1, slot], sibling)
        )

    def txt_step(step):
        up, down = (step - 1, step, 1), ((9 - step) % 8, 8 - step, -1)
        for (at, to, way), half in ((up, 0), (down, 1), (up, 1), (down, 0)):
            if at != 0:
                txt_copies[at, half].wait_recv()
            if to != 4 or half == (way < 0):
                rows = pl.ds(half * 16, 16)
                txt_copies[to, half] = send(
                    v.txt.at[0, at, rows],
                    v.txt.at[0, to, rows],
                    v.txt_sem.at[0, to, half],
                    v.txt_sem.at[1, to, half],
                    to_z(way),
                )
        for at in {up[0], down[0]}:
            share(at)

    txt_step(1)

    unit = embed(0)
    v.img[0, 0, 0] = unit[:16]
    v.img[1, 0, 0] = unit[16:]
    ways = (to_x, to_y)

    def image_push(at, to, phase, half, k, way):
        sem = v.img_sem
        return send(
            v.img.at[at], v.img.at[to], sem.at[0, phase, half, k], sem.at[1, phase, half, k], way(k)
        )

    img_first = ([], [])
    img_copies = []
    for k in (2, 1, 3):
        for half in range(2):
            img_first[half].append(image_push((half, 0, 0), (half, 0, k), 0, half, k, ways[half]))
    for k in (2, 1, 3):
        for half in range(2):
            img_copies.append(image_push((half, 0, 0), (half, k, 0), 1, half, k, ways[1 - half]))

    txt_step(2)
    txt_step(3)
    turned = pl.ds(1, 3)
    for half in range(2):
        await_all(img_first[half])
        for k in (2, 1, 3):
            img_copies.append(
                image_push((half, 0, turned), (half, k, turned), 2, half, k, ways[1 - half])
            )
    txt_step(4)
    await_all(txt_copies[4, half] for half in range(2))
    share(4)
    await_all(stream_ring)
    stream_ring = stream_step(3)
    await_all(img_copies)

    scale, shift = scale_ref[0], shift_ref[0]
    row_id = lax.broadcasted_iota(jnp.int32, (256, 256), 0)
    col_id = lax.broadcasted_iota(jnp.int32, (256, 256), 1)

    def pair_coefficients(core):
        @pl.loop(0, 2, unroll=True)
        def _(half):
            inner = lax.dot_general(
                v.img[half].reshape(256, 1536),
                v.txt[core].reshape(256, 1536),
                (((1,), (1,)), ((), ())),
                preferred_element_type=F32,
            )
            value = jax.nn.sigmoid(scale * inner + shift)
            if core == 0:
                positive = (row_id < 16) & (row_id + half * 16 == col_id)
                value = value - positive.astype(F32)
            value = scale * value
            v.coef[half, :, core * 256 : core * 256 + 256] = value.astype(BF16)
            v.coef_t[core, :, pl.ds(pl.multiple_of(half * 256, 256), 256)] = value.T.astype(BF16)

    pair_coefficients(0)
    await_all(pair_copies)
    pair_coefficients(1)

    def text_partials(core):
        @pl.loop(0, 6, unroll=True)
        def _(f):
            cols = pl.ds(pl.multiple_of(f * 256, 256), 256)
            product = jnp.dot(
                v.coef_t[core], v.img[:, :, :, :, cols].reshape(512, 256), preferred_element_type=F32
            ).reshape(8, 32, 256)
            if core == 0:
                v.gt_own[:, :, cols] = product
            else:
                v.gt_out[:, :, cols] = product.astype(BF16)

    def image_partials(half):
        @pl.loop(0, 6, unroll=True)
        def _(f):
            cols = pl.ds(pl.multiple_of(f * 256, 256), 256)
            product = jnp.dot(
                v.coef[half], v.txt[:, :, :, cols].reshape(512, 256), preferred_element_type=F32
            )
            v.gi_out[half, :, :, :, cols] = product.reshape(4, 4, 16, 256).astype(BF16)

    gi_first, gi_copies = ([], []), ([], [])

    def image_start(half):
        image_partials(half)
        for phase, blocks, copies in ((0, turned, gi_first), (2, pl.ds(0, 1), gi_copies)):
            for k in (2, 1, 3):
                copies[half].append(
                    send(
                        v.gi_out.at[half, k, blocks],
                        v.gi_in.at[half, k, blocks],
                        v.gi_sem.at[0, phase, half, k],
                        v.gi_sem.at[1, phase, half, k],
                        ways[1 - half](-k),
                    )
                )

    gh_copies = ([], [])

    def image_own(half, k):
        total = v.gi_out[half, 0, k].astype(F32)
        for j in range(1, 4):
            total += v.gi_in[half, j, k].astype(F32)
        return total

    def image_middle(half):
        await_all(gi_first[half])
        for k in (2, 1, 3):
            v.gh_out[half, k] = image_own(half, k).astype(BF16)
            gh_copies[half].append(
                send(
                    v.gh_out.at[half, k],
                    v.gh_in.at[half, k],
                    v.gi_sem.at[0, 1, half, k],
                    v.gi_sem.at[1, 1, half, k],
                    ways[half](-k),
                )
            )

    def image_end(half):
        await_all(gi_copies[half])
        total = image_own(half, 0)
        await_all(gh_copies[half])
        for k in range(1, 4):
            total += v.gh_in[half, k].astype(F32)
        return total

    gz_copies = {}

    def text_own(r, half):
        rows = slice(half * 16, half * 16 + 16)
        return v.gt_own[r, rows] + v.gt_in[r, rows].astype(F32)

    def text_step(step):
        moves = [(5 - step, 0, -1), (3 + step, 1, 1)]
        if step < 4:
            moves += [(4 - step, 1, -1), (4 + step, 0, 1)]
        for r, half, way in moves:
            rows = slice(half * 16, half * 16 + 16)
            total = text_own(r, half)
            before = r - way
            if (before, half) in gz_copies and (before != 4 or half == (way > 0)):
                gz_copies[before, half].wait_recv()
                total += v.gz_in[before, rows].astype(F32)
            v.gz_out[r, rows] = total.astype(BF16)
            gz_copies[r, half] = send(
                v.gz_out.at[r, pl.ds(half * 16, 16)],
                v.gz_in.at[r, pl.ds(half * 16, 16)],
                v.gz_sem.at[0, r, half],
                v.gz_sem.at[1, r, half],
                to_z(way),
            )

    def text_end(half):
        rows = slice(half * 16, half * 16 + 16)
        total = text_own(0, half)
        for r in (1, 7):
            gz_copies[r, half].wait_recv()
            total += v.gz_in[r, rows].astype(F32)
        return total

    text_partials(1)
    gt_copy = send(v.gt_out, v.gt_in, v.gt_sem.at[0], v.gt_sem.at[1], sibling)
    image_start(0)
    image_start(1)
    text_partials(0)
    gt_copy.wait_recv()
    text_step(1)
    text_step(2)
    text_step(3)
    image_middle(0)
    image_middle(1)
    text_step(4)

    turn_copies = ([], [])

    def turn(tower, grad):
        raw = raw_gradient(grad, v.unit[tower], v.norm[tower][:, :1])
        for k in range(8):
            cols = slice(k * 192, k * 192 + 192)
            v.pack[tower, k] = jnp.concatenate([raw[:16, cols], raw[16:, cols]], axis=1)
        v.graw[tower, t, 0] = v.pack[tower, z]
        for k in range(1, 8):
            turn_copies[tower].append(
                send(
                    v.pack.at[tower, (z + k) % 8],
                    v.graw.at[tower, t, k],
                    v.turn_sem.at[0, tower, k],
                    v.turn_sem.at[1, tower, k],
                    to_z(k),
                )
            )

    turn(1, jnp.concatenate([text_end(half) for half in range(2)], axis=0))
    turn(0, jnp.concatenate([image_end(half) for half in range(2)], axis=0))

    spread_copies, low_copies, high_copies = ([], []), {}, {}

    low_slots, high_slots = pl.ds(0, 3), pl.ds(3, 5)

    def spread(tower, owner, slots, phase, j, peer):
        block = v.graw.at[tower, owner, slots]
        sem = v.spread_sem
        return send(block, block, sem.at[0, tower, phase, j], sem.at[1, tower, phase, j], peer)

    def spread_start(tower):
        await_all(turn_copies[tower][:2])
        low_copies[tower] = spread(tower, t, low_slots, 0, 0, partner)
        await_all(turn_copies[tower][2:])
        high_copies[tower] = [spread(tower, t, high_slots, 0, k, to_y(k)) for k in range(1, 4)]
        spread_copies[tower].append(spread(tower, t, high_slots, 1, 0, partner))
        spread_copies[tower].extend(
            spread(tower, t, low_slots, 1, k, to_y(k)) for k in range(1, 4)
        )

    def spread_end(tower):
        low_copies[tower].wait_recv()
        for k in range(1, 4):
            spread_copies[tower].append(
                spread(tower, (t + 4) % 8, low_slots, 2, k, to_y(k))
            )
        for k in (1, 3, 2):
            high_copies[tower][k - 1].wait_recv()
            owner = low * 4 + (y - k) % 4
            spread_copies[tower].append(spread(tower, owner, high_slots, 2, k + 4, partner))

    def contract(tower):
        await_all(spread_copies[tower])
        totals = [jnp.zeros((192, 256), F32)] * 2
        for r in range(0, 8, 2):
            rows = jnp.concatenate([v.graw[tower, :, r + i].reshape(128, 384) for i in range(2)], axis=0)
            for half in range(2):
                lanes = slice(half * 128, half * 128 + 128)
                columns = jnp.concatenate([v.stream[r + i, tower, :, lanes] for i in range(2)], axis=1)
                totals[half] += jnp.dot(
                    columns, rows[:, half * 128 : half * 128 + 256], preferred_element_type=F32
                )
        return (totals[0][:, :192] + totals[1][:, 64:]).T

    await_all(stream_ring)
    stream_ring = stream_step(4)
    spread_start(first)
    spread_start(second)
    spread_end(first)
    spread_end(second)
    await_all(stream_ring)
    text_sum = contract(1)
    sums = jnp.concatenate([contract(0), text_sum], axis=1)
    for q in range(4):
        v.part[q % 2, q // 2] = sums[q * 48 : q * 48 + 48]

    core_copy = send(v.part.at[1 - c], v.part_in, v.part_sem.at[0, 0], v.part_sem.at[1, 0], sibling)
    high = x // 2
    core_copy.wait_recv()
    v.last_out[...] = v.part[c, 1 - high] + v.part_in[1 - high]
    last_copy = send(
        v.last_out, v.last_in, v.part_sem.at[0, 1], v.part_sem.at[1, 1], device(z, (x + 2) % 4, y, c)
    )
    total = v.part[c, high] + v.part_in[high]
    last_copy.wait_recv()
    output[...] = total + v.last_in[...]
    for copy in sends:
        copy.wait_send()


def on_device(
    picture_skip_entries,
    picture_activations,
    picture_contract_weights,
    picture_embedding_map,
    caption_skip_entries,
    caption_activations,
    caption_contract_weights,
    caption_embedding_map,
    sharpness_coefficient,
    pairwise_score_shift,
):
    both = pl.pallas_call(
        window_kernel,
        out_shape=jax.ShapeDtypeStruct((48, 384), F32),
        in_specs=[pl.BlockSpec(memory_space=pl.ANY)] * 8
        + [pl.BlockSpec(memory_space=pltpu.SMEM)] * 2,
        out_specs=pl.BlockSpec(memory_space=pltpu.VMEM),
        scratch_shapes=[*SCRATCH.values(), *DOWN.values(), *EMB.values()],
        compiler_params=pltpu.CompilerParams(
            collective_id=0, has_side_effects=True, vmem_limit_bytes=VMEM_LIMIT
        ),
    )(
        picture_activations,
        picture_contract_weights,
        picture_embedding_map,
        picture_skip_entries.T,
        caption_activations,
        caption_contract_weights,
        caption_embedding_map,
        caption_skip_entries.T,
        sharpness_coefficient,
        pairwise_score_shift,
    )
    return both[:, :192].T, both[:, 192:].T


def solution(mesh):
    placed = (
        P("dp", "tensor"),
        P("dp", "tensor"),
        P("tensor", None),
        P("tensor", None),
        P("dp", "tensor"),
        P("dp", "tensor"),
        P("tensor", None),
        P("tensor", None),
        P(),
        P(),
    )
    return jax.shard_map(
        on_device,
        mesh=mesh,
        in_specs=placed,
        out_specs=(P("tensor", "dp"), P("tensor", "dp")),
        check_vma=False,
    )
```

time: 849 us -> 103 us (0.12)
  waiting for transfers between devices: 529 us -> 0 us
  matrix products: 190 us -> 0 us
  Pallas kernels: 0 us -> 99.6 us
  blocking collectives: 72.8 us -> 0 us
  starting transfers between devices: 25.5 us -> 0 us
  between operations: 14.3 us -> 1.93 us
    reduce_scatter x7 -> x0, waiting for transfers between devices: 362 us -> none  [the longest x1 120 us: on_device(): lax.psum_scatter(term_image, 'dp', scatter_dimension=1, tiled=True)]
    dot_general x102 -> x0, matrix products: 190 us -> none  [the longest x32 93.1 us: image_term(): lax.dot_general(pair_coef, text_rows, (((0,), (0,)), ((), ())), preferred...]
    ppermute x64 -> x0, waiting for transfers between devices: 167 us -> none  [from_behind(): return lax.ppermute(block, axis, route)]
    pallas_call x0 -> x1, Pallas kernels: none -> 99.6 us  [on_device(): pl.pallas_call(window_kernel, out_shape=jax.ShapeDtypeStruct((48, 384), F...]
    all_gather x3 -> x0, blocking collectives: 72.8 us -> none  [the longest x1 25.3 us: on_device(): lax.all_gather(raw_gradient(text_grad, unit_text, norm_text), 'tensor', a...]
    ppermute x64 -> x0, starting transfers between devices: 25.2 us -> none  [from_behind(): return lax.ppermute(block, axis, route)]
  transfers between devices with their start and end apart: 71 -> 0, of which waited for: 66 -> 0; matrix products, arithmetic and copies ran while one was open for 23% -> 0% of each run, Pallas kernels for 0% -> 0%
where the time goes in v1:
time: 103 us
  Pallas kernels  99.6 us (97%)
  between operations  1.93 us (2%)
  local copies, waits for them, and re-layouts  1.58 us (2%)
    pallas_call x1, Pallas kernels, on_device(): pl.pallas_call(window_kernel, out_shape=jax.ShapeDtypeStruct((48, 384), F...  99.6 us

profile of v1, /device:TPU:1, one launch (start us, length us, event | category | flops | bytes accessed | tf_op | source)
XLA Modules:
  0.0 103.1 jit_solution(3625766195928381919)
XLA Ops:
  1.9 99.6 %shard_map.113 = f32[48,384]{1,0:T(8,128)} custom-call(bf16[256,768]{1,0:T(8,128)(2,1)} %refs_0_.1, bf16[768,1536]{1,0:T(8,128)(2,1)} %refs_1_.1, bf16[192,1536]{1,0:T(8,128)(2,1)} %refs_2_.1, bf16[192,256]{1,0:T(8,128)(2,1)} %bitcast.6, bf16[256,768]{1,0:T(8,128)(2,1)} %refs_4_.1, bf16[768,1536]{1,0:T(8,128)(2,1)} %refs_5_.1, bf16[192,1536]{1,0:T(8,128)(2,1)} %refs_6_.1, ...), custom_call_target="tpu_custom_call" | custom-call | tf_op jit(solution)/shard_map/pallas_call | solution.py:618
  101.5 1.6 %slice_bitcast_fusion = (f32[192,48]{0,1:T(8,128)}, f32[192,48]{0,1:T(8,128)}) fusion(f32[48,384]{1,0:T(8,128)} %shard_map.113), kind=kLoop, calls=%fused_computation | loop fusion | bytes 147456 | tf_op jit(solution)/shard_map/transpose | solution.py:640

commit v2 on v1

--- a/solution.py
+++ b/solution.py
@@ -69,21 +69,19 @@
     gh_in=pltpu.VMEM((2, 4, 16, 1536), BF16),
     pack=pltpu.VMEM((2, 8, 16, 384), BF16),
     graw=pltpu.VMEM((2, 8, 8, 16, 384), BF16),
-    part=pltpu.VMEM((2, 2, 48, 384), F32),
-    part_in=pltpu.VMEM((2, 48, 384), F32),
-    last_out=pltpu.VMEM((48, 384), F32),
-    last_in=pltpu.VMEM((48, 384), F32),
+    part=pltpu.VMEM((2, 4, 48, 256), F32),
+    part_in=pltpu.VMEM((2, 4, 48, 256), F32),
     load_sem=pltpu.SemaphoreType.DMA((2, 7)),
     stream_sem=pltpu.SemaphoreType.DMA((2, 9)),
     img_sem=pltpu.SemaphoreType.DMA((2, 3, 2, 4)),
     txt_sem=pltpu.SemaphoreType.DMA((2, 8, 2)),
     pair_sem=pltpu.SemaphoreType.DMA((2, 8)),
-    gt_sem=pltpu.SemaphoreType.DMA((2,)),
+    gt_sem=pltpu.SemaphoreType.DMA((2, 3)),
     gz_sem=pltpu.SemaphoreType.DMA((2, 8, 2)),
     gi_sem=pltpu.SemaphoreType.DMA((2, 3, 2, 4)),
     turn_sem=pltpu.SemaphoreType.DMA((2, 2, 8)),
     spread_sem=pltpu.SemaphoreType.DMA((2, 2, 3, 8)),
-    part_sem=pltpu.SemaphoreType.DMA((2, 2)),
+    part_sem=pltpu.SemaphoreType.DMA((2, 2, 4)),
 )
 
 
@@ -97,12 +95,17 @@
         s.relay, s.cross, s.near, s.last, s.along, s.wide = ({} for _ in range(6))
     d, t = lax.axis_index("dp"), lax.axis_index("tensor")
     z, x, y, c = d // 4, d // 2 % 2 * 2 + t // 4, t % 4, d % 2
-    sends = []
+    sends, settled = [], [0]
 
     def send(*args):
         copy = push(*args)
         sends.append(copy)
         return copy
+
+    def settle(mark):
+        for copy in sends[settled[0] : mark]:
+            copy.wait_send()
+        settled[0] = max(settled[0], mark)
 
     def to_x(k):
         return device(z, (x + k) % 4, y, c)
@@ -133,7 +136,7 @@
     peers = [(d, (t + k) % 8) for k in range(1, 8)]
     peers += [to_z(k) for k in range(1, 8)]
     peers += [device(z, (x + 2) % 4, y, c), device(z, (x // 2 * 2 + 2) % 4 + 1 - x % 2, y, c)]
-    peers += [sibling]
+    peers += [sibling, device(z, (x + 2) % 4, y, 1 - c)]
     barrier = pltpu.get_barrier_semaphore()
     for peer in peers:
         pl.semaphore_signal(barrier, inc=1, device_id=peer, device_id_type=MESH)
@@ -309,6 +312,7 @@
         v.norm[tower] = jnp.broadcast_to(norm, (32, 128))
         return unit.astype(BF16)
 
+    mark = len(sends)
     v.txt[0, 0] = embed(1)
     pair_copies = []
     txt_copies = {}
@@ -348,14 +352,13 @@
             v.img.at[at], v.img.at[to], sem.at[0, phase, half, k], sem.at[1, phase, half, k], way(k)
         )
 
-    img_first = ([], [])
-    img_copies = []
+    img_first, img_copies = ([], []), {1: [], 2: [], 3: []}
     for k in (2, 1, 3):
         for half in range(2):
             img_first[half].append(image_push((half, 0, 0), (half, 0, k), 0, half, k, ways[half]))
     for k in (2, 1, 3):
         for half in range(2):
-            img_copies.append(image_push((half, 0, 0), (half, k, 0), 1, half, k, ways[1 - half]))
+            img_copies[k].append(image_push((half, 0, 0), (half, k, 0), 1, half, k, ways[1 - half]))
 
     txt_step(2)
     txt_step(3)
@@ -363,40 +366,50 @@
     for half in range(2):
         await_all(img_first[half])
         for k in (2, 1, 3):
-            img_copies.append(
+            img_copies[k].append(
                 image_push((half, 0, turned), (half, k, turned), 2, half, k, ways[1 - half])
             )
     txt_step(4)
+    settle(mark)
     await_all(txt_copies[4, half] for half in range(2))
     share(4)
     await_all(stream_ring)
     stream_ring = stream_step(3)
-    await_all(img_copies)
+    mark = len(sends)
 
     scale, shift = scale_ref[0], shift_ref[0]
     row_id = lax.broadcasted_iota(jnp.int32, (256, 256), 0)
     col_id = lax.broadcasted_iota(jnp.int32, (256, 256), 1)
 
-    def pair_coefficients(core):
-        @pl.loop(0, 2, unroll=True)
-        def _(half):
-            inner = lax.dot_general(
-                v.img[half].reshape(256, 1536),
-                v.txt[core].reshape(256, 1536),
-                (((1,), (1,)), ((), ())),
-                preferred_element_type=F32,
-            )
-            value = jax.nn.sigmoid(scale * inner + shift)
-            if core == 0:
-                positive = (row_id < 16) & (row_id + half * 16 == col_id)
-                value = value - positive.astype(F32)
-            value = scale * value
-            v.coef[half, :, core * 256 : core * 256 + 256] = value.astype(BF16)
-            v.coef_t[core, :, pl.ds(pl.multiple_of(half * 256, 256), 256)] = value.T.astype(BF16)
-
-    pair_coefficients(0)
+    own_pair = ((row_id < 16) & (col_id == row_id)) | (
+        (row_id >= 128) & (row_id < 144) & (col_id == row_id - 112)
+    )
+
+    def pair_coefficients(core, group):
+        inner = lax.dot_general(
+            v.img[:, 2 * group : 2 * group + 2].reshape(256, 1536),
+            v.txt[core].reshape(256, 1536),
+            (((1,), (1,)), ((), ())),
+            preferred_element_type=F32,
+        )
+        value = jax.nn.sigmoid(scale * inner + shift)
+        if core == 0 and group == 0:
+            value = value - own_pair.astype(F32)
+        value = scale * value
+        turned_value = value.T.astype(BF16)
+        value = value.astype(BF16)
+        for half in range(2):
+            part = slice(half * 128, half * 128 + 128)
+            start = group * 128
+            v.coef[half, start : start + 128, core * 256 : core * 256 + 256] = value[part]
+            v.coef_t[core, :, half * 256 + start : half * 256 + start + 128] = turned_value[:, part]
+
+    await_all(img_copies[1] + img_copies[2] + img_copies[3])
+    pair_coefficients(0, 0)
+    pair_coefficients(0, 1)
     await_all(pair_copies)
-    pair_coefficients(1)
+    pair_coefficients(1, 0)
+    pair_coefficients(1, 1)
 
     def text_partials(core):
         @pl.loop(0, 6, unroll=True)
@@ -500,19 +513,27 @@
         return total
 
     text_partials(1)
-    gt_copy = send(v.gt_out, v.gt_in, v.gt_sem.at[0], v.gt_sem.at[1], sibling)
+    gt_copies = []
+    for j, (start, count) in enumerate(((3, 3), (0, 3), (6, 2))):
+        part = pl.ds(start, count)
+        gt_copies.append(
+            send(v.gt_out.at[part], v.gt_in.at[part], v.gt_sem.at[0, j], v.gt_sem.at[1, j], sibling)
+        )
+    text_partials(0)
     image_start(0)
+    gt_copies[0].wait_recv()
+    text_step(1)
     image_start(1)
-    text_partials(0)
-    gt_copy.wait_recv()
-    text_step(1)
+    await_all(gt_copies[1:])
+    settle(mark)
     text_step(2)
     text_step(3)
     image_middle(0)
     image_middle(1)
     text_step(4)
-
-    turn_copies = ([], [])
+    mark = len(sends)
+
+    turn_copies = ({}, {})
 
     def turn(tower, grad):
         raw = raw_gradient(grad, v.unit[tower], v.norm[tower][:, :1])
@@ -520,15 +541,13 @@
             cols = slice(k * 192, k * 192 + 192)
             v.pack[tower, k] = jnp.concatenate([raw[:16, cols], raw[16:, cols]], axis=1)
         v.graw[tower, t, 0] = v.pack[tower, z]
-        for k in range(1, 8):
-            turn_copies[tower].append(
-                send(
-                    v.pack.at[tower, (z + k) % 8],
-                    v.graw.at[tower, t, k],
-                    v.turn_sem.at[0, tower, k],
-                    v.turn_sem.at[1, tower, k],
-                    to_z(k),
-                )
+        for k in (4, 3, 5, 2, 6, 1, 7):
+            turn_copies[tower][k] = send(
+                v.pack.at[tower, (z + k) % 8],
+                v.graw.at[tower, t, k],
+                v.turn_sem.at[0, tower, k],
+                v.turn_sem.at[1, tower, k],
+                to_z(k),
             )
 
     turn(1, jnp.concatenate([text_end(half) for half in range(2)], axis=0))
@@ -544,23 +563,25 @@
         return send(block, block, sem.at[0, tower, phase, j], sem.at[1, tower, phase, j], peer)
 
     def spread_start(tower):
-        await_all(turn_copies[tower][:2])
+        await_all(turn_copies[tower][k] for k in (1, 2))
         low_copies[tower] = spread(tower, t, low_slots, 0, 0, partner)
-        await_all(turn_copies[tower][2:])
-        high_copies[tower] = [spread(tower, t, high_slots, 0, k, to_y(k)) for k in range(1, 4)]
+        await_all(turn_copies[tower][k] for k in range(3, 8))
+        high_copies[tower] = {
+            k: spread(tower, t, high_slots, 0, k, to_y(k)) for k in (2, 1, 3)
+        }
         spread_copies[tower].append(spread(tower, t, high_slots, 1, 0, partner))
         spread_copies[tower].extend(
-            spread(tower, t, low_slots, 1, k, to_y(k)) for k in range(1, 4)
+            spread(tower, t, low_slots, 1, k, to_y(k)) for k in (2, 1, 3)
         )
 
     def spread_end(tower):
         low_copies[tower].wait_recv()
-        for k in range(1, 4):
+        for k in (2, 1, 3):
             spread_copies[tower].append(
                 spread(tower, (t + 4) % 8, low_slots, 2, k, to_y(k))
             )
         for k in (1, 3, 2):
-            high_copies[tower][k - 1].wait_recv()
+            high_copies[tower][k].wait_recv()
             owner = low * 4 + (y - k) % 4
             spread_copies[tower].append(spread(tower, owner, high_slots, 2, k + 4, partner))
 
@@ -575,32 +596,45 @@
                 totals[half] += jnp.dot(
                     columns, rows[:, half * 128 : half * 128 + 256], preferred_element_type=F32
                 )
-        return (totals[0][:, :192] + totals[1][:, 64:]).T
+        total = totals[0][:, :192] + totals[1][:, 64:]
+        return jnp.concatenate([total, jnp.zeros((64, 192), F32)], axis=0).T
 
     await_all(stream_ring)
     stream_ring = stream_step(4)
     spread_start(first)
     spread_start(second)
+    settle(mark)
     spread_end(first)
     spread_end(second)
+    mark = len(sends)
     await_all(stream_ring)
-    text_sum = contract(1)
-    sums = jnp.concatenate([contract(0), text_sum], axis=1)
-    for q in range(4):
-        v.part[q % 2, q // 2] = sums[q * 48 : q * 48 + 48]
-
-    core_copy = send(v.part.at[1 - c], v.part_in, v.part_sem.at[0, 0], v.part_sem.at[1, 0], sibling)
-    high = x // 2
-    core_copy.wait_recv()
-    v.last_out[...] = v.part[c, 1 - high] + v.part_in[1 - high]
-    last_copy = send(
-        v.last_out, v.last_in, v.part_sem.at[0, 1], v.part_sem.at[1, 1], device(z, (x + 2) % 4, y, c)
-    )
-    total = v.part[c, high] + v.part_in[high]
-    last_copy.wait_recv()
-    output[...] = total + v.last_in[...]
-    for copy in sends:
-        copy.wait_send()
+
+    part_copies = ([], [])
+    for tower in (first, second):
+        columns = contract(tower)
+        for q in range(4):
+            v.part[tower, q] = columns[q * 48 : q * 48 + 48]
+        for k in (3, 2, 1):
+            x_to, c_to = (x + k // 2 * 2) % 4, (c + k) % 2
+            part_copies[tower].append(
+                send(
+                    v.part.at[tower, x_to // 2 * 2 + c_to],
+                    v.part_in.at[tower, k],
+                    v.part_sem.at[0, tower, k],
+                    v.part_sem.at[1, tower, k],
+                    device(z, x_to, y, c_to),
+                )
+            )
+    settle(mark)
+    totals = {}
+    for tower in (first, second):
+        total = v.part[tower, d % 4]
+        for k in (1, 2, 3):
+            part_copies[tower][3 - k].wait_recv()
+            total += v.part_in[tower, k]
+        totals[tower] = total[:, :192]
+    output[...] = jnp.concatenate([totals[0], totals[1]], axis=1)
+    settle(len(sends))
 
 
 def on_device(

time: 103 us -> 104 us (level)
  no operation moved by 1% of the time
where the time goes in v2:
time: 104 us
  Pallas kernels  100 us (96%)
  between operations  1.93 us (2%)
  local copies, waits for them, and re-layouts  1.58 us (2%)
    pallas_call x1, Pallas kernels, on_device(): pl.pallas_call(window_kernel, out_shape=jax.ShapeDtypeStruct((48, 384), F...  100 us

profile of v2, /device:TPU:1, one launch (start us, length us, event | category | flops | bytes accessed | tf_op | source)
XLA Modules:
  0.0 103.8 jit_solution(14335719212131015361)
XLA Ops:
  1.9 100.3 %shard_map.113 = f32[48,384]{1,0:T(8,128)} custom-call(bf16[256,768]{1,0:T(8,128)(2,1)} %refs_0_.1, bf16[768,1536]{1,0:T(8,128)(2,1)} %refs_1_.1, bf16[192,1536]{1,0:T(8,128)(2,1)} %refs_2_.1, bf16[192,256]{1,0:T(8,128)(2,1)} %bitcast.6, bf16[256,768]{1,0:T(8,128)(2,1)} %refs_4_.1, bf16[768,1536]{1,0:T(8,128)(2,1)} %refs_5_.1, bf16[192,1536]{1,0:T(8,128)(2,1)} %refs_6_.1, ...), custom_call_target="tpu_custom_call" | custom-call | tf_op jit(solution)/shard_map/pallas_call | solution.py:652
  102.2 1.6 %slice_bitcast_fusion = (f32[192,48]{0,1:T(8,128)}, f32[192,48]{0,1:T(8,128)}) fusion(f32[48,384]{1,0:T(8,128)} %shard_map.113), kind=kLoop, calls=%fused_computation | loop fusion | bytes 147456 | tf_op jit(solution)/shard_map/transpose | solution.py:674

commit v3 on v2

--- a/solution.py
+++ b/solution.py
@@ -72,7 +72,7 @@
     part=pltpu.VMEM((2, 4, 48, 256), F32),
     part_in=pltpu.VMEM((2, 4, 48, 256), F32),
     load_sem=pltpu.SemaphoreType.DMA((2, 7)),
-    stream_sem=pltpu.SemaphoreType.DMA((2, 9)),
+    stream_sem=pltpu.SemaphoreType.DMA((2, 8, 2)),
     img_sem=pltpu.SemaphoreType.DMA((2, 3, 2, 4)),
     txt_sem=pltpu.SemaphoreType.DMA((2, 8, 2)),
     pair_sem=pltpu.SemaphoreType.DMA((2, 8)),
@@ -271,17 +271,21 @@
         for copy in copies:
             copy.wait_recv()
 
-    def stream_step(step):
+    def stream_push(at, to, tower, way):
+        sem = v.stream_sem
+        return send(
+            v.stream.at[at, tower],
+            v.stream.at[to, tower],
+            sem.at[0, to, tower],
+            sem.at[1, to, tower],
+            to_z(way),
+        )
+
+    def stream_step(step, tower):
         if step < 4:
-            ways = ((1, (step - 1,), (step,), step), (-1, ((9 - step) % 8,), (8 - step,), 8 - step))
-        else:
-            ways = ((1, (3, 0), (4, 0), 4), (-1, (5, 1), (4, 1), 8))
-        return [
-            send(
-                v.stream.at[at], v.stream.at[to], v.stream_sem.at[0, j], v.stream_sem.at[1, j], to_z(way)
-            )
-            for way, at, to, j in ways
-        ]
+            up = stream_push(step - 1, step, tower, 1)
+            return [up, stream_push((9 - step) % 8, 8 - step, tower, -1)]
+        return [stream_push(3, 4, 0, 1) if tower == 0 else stream_push(5, 4, 1, -1)]
 
     first, second = 1, 0
     down_projection(first)
@@ -292,17 +296,24 @@
     scatter_wide(v.down, first)
     scatter_along(v.down, second)
     scatter_wide(v.down, second)
+    stream_ring = {}
     embedding_projection(first)
+    stream_ring[first] = stream_step(1, first)
     embedding_projection(second)
-    stream_ring = stream_step(1)
+    stream_ring[second] = stream_step(1, second)
+
+    def stream_next(step, tower):
+        await_all(stream_ring[tower])
+        stream_ring[tower] = stream_step(step, tower)
+
     scatter_relay(v.emb, first)
     scatter_along(v.emb, first)
     scatter_relay(v.emb, second)
+    stream_next(2, first)
     scatter_wide(v.emb, first)
+    stream_next(2, second)
     scatter_along(v.emb, second)
     scatter_wide(v.emb, second)
-    await_all(stream_ring)
-    stream_ring = stream_step(2)
 
     def embed(tower):
         raw = scatter_end(v.emb, tower, 1)
@@ -373,8 +384,8 @@
     settle(mark)
     await_all(txt_copies[4, half] for half in range(2))
     share(4)
-    await_all(stream_ring)
-    stream_ring = stream_step(3)
+    stream_next(3, first)
+    stream_next(3, second)
     mark = len(sends)
 
     scale, shift = scale_ref[0], shift_ref[0]
@@ -599,15 +610,15 @@
         total = totals[0][:, :192] + totals[1][:, 64:]
         return jnp.concatenate([total, jnp.zeros((64, 192), F32)], axis=0).T
 
-    await_all(stream_ring)
-    stream_ring = stream_step(4)
+    stream_next(4, first)
+    stream_next(4, second)
     spread_start(first)
     spread_start(second)
     settle(mark)
     spread_end(first)
     spread_end(second)
     mark = len(sends)
-    await_all(stream_ring)
+    await_all(stream_ring[first] + stream_ring[second])
 
     part_copies = ([], [])
     for tower in (first, second):

time: 104 us -> 104 us (level)
  no operation moved by 1% of the time
where the time goes in v3:
time: 104 us
  Pallas kernels  100 us (96%)
  between operations  1.93 us (2%)
  local copies, waits for them, and re-layouts  1.58 us (2%)
    pallas_call x1, Pallas kernels, on_device(): pl.pallas_call(window_kernel, out_shape=jax.ShapeDtypeStruct((48, 384), F...  100 us

profile of v3, /device:TPU:1, one launch (start us, length us, event | category | flops | bytes accessed | tf_op | source)
XLA Modules:
  0.0 103.8 jit_solution(15141655490230631212)
XLA Ops:
  1.9 100.3 %shard_map.113 = f32[48,384]{1,0:T(8,128)} custom-call(bf16[256,768]{1,0:T(8,128)(2,1)} %refs_0_.1, bf16[768,1536]{1,0:T(8,128)(2,1)} %refs_1_.1, bf16[192,1536]{1,0:T(8,128)(2,1)} %refs_2_.1, bf16[192,256]{1,0:T(8,128)(2,1)} %bitcast.6, bf16[256,768]{1,0:T(8,128)(2,1)} %refs_4_.1, bf16[768,1536]{1,0:T(8,128)(2,1)} %refs_5_.1, bf16[192,1536]{1,0:T(8,128)(2,1)} %refs_6_.1, ...), custom_call_target="tpu_custom_call" | custom-call | tf_op jit(solution)/shard_map/pallas_call | solution.py:663
  102.2 1.6 %slice_bitcast_fusion = (f32[192,48]{0,1:T(8,128)}, f32[192,48]{0,1:T(8,128)}) fusion(f32[48,384]{1,0:T(8,128)} %shard_map.113), kind=kLoop, calls=%fused_computation | loop fusion | bytes 147456 | tf_op jit(solution)/shard_map/transpose | solution.py:685

commit v4 on v3

--- a/solution.py
+++ b/solution.py
@@ -69,8 +69,10 @@
     gh_in=pltpu.VMEM((2, 4, 16, 1536), BF16),
     pack=pltpu.VMEM((2, 8, 16, 384), BF16),
     graw=pltpu.VMEM((2, 8, 8, 16, 384), BF16),
-    part=pltpu.VMEM((2, 4, 48, 256), F32),
-    part_in=pltpu.VMEM((2, 4, 48, 256), F32),
+    part=pltpu.VMEM((2, 2, 2, 48, 256), F32),
+    part_in=pltpu.VMEM((2, 2, 48, 256), F32),
+    last_out=pltpu.VMEM((2, 48, 256), F32),
+    last_in=pltpu.VMEM((2, 48, 256), F32),
     load_sem=pltpu.SemaphoreType.DMA((2, 7)),
     stream_sem=pltpu.SemaphoreType.DMA((2, 8, 2)),
     img_sem=pltpu.SemaphoreType.DMA((2, 3, 2, 4)),
@@ -81,7 +83,7 @@
     gi_sem=pltpu.SemaphoreType.DMA((2, 3, 2, 4)),
     turn_sem=pltpu.SemaphoreType.DMA((2, 2, 8)),
     spread_sem=pltpu.SemaphoreType.DMA((2, 2, 3, 8)),
-    part_sem=pltpu.SemaphoreType.DMA((2, 2, 4)),
+    part_sem=pltpu.SemaphoreType.DMA((2, 2, 2)),
 )
 
 
@@ -136,7 +138,7 @@
     peers = [(d, (t + k) % 8) for k in range(1, 8)]
     peers += [to_z(k) for k in range(1, 8)]
     peers += [device(z, (x + 2) % 4, y, c), device(z, (x // 2 * 2 + 2) % 4 + 1 - x % 2, y, c)]
-    peers += [sibling, device(z, (x + 2) % 4, y, 1 - c)]
+    peers += [sibling]
     barrier = pltpu.get_barrier_semaphore()
     for peer in peers:
         pl.semaphore_signal(barrier, inc=1, device_id=peer, device_id_type=MESH)
@@ -620,30 +622,34 @@
     mark = len(sends)
     await_all(stream_ring[first] + stream_ring[second])
 
-    part_copies = ([], [])
+    high = x // 2
+    core_copies, last_copies, totals = {}, {}, {}
     for tower in (first, second):
         columns = contract(tower)
         for q in range(4):
-            v.part[tower, q] = columns[q * 48 : q * 48 + 48]
-        for k in (3, 2, 1):
-            x_to, c_to = (x + k // 2 * 2) % 4, (c + k) % 2
-            part_copies[tower].append(
-                send(
-                    v.part.at[tower, x_to // 2 * 2 + c_to],
-                    v.part_in.at[tower, k],
-                    v.part_sem.at[0, tower, k],
-                    v.part_sem.at[1, tower, k],
-                    device(z, x_to, y, c_to),
-                )
-            )
+            v.part[tower, q % 2, q // 2] = columns[q * 48 : q * 48 + 48]
+        core_copies[tower] = send(
+            v.part.at[tower, 1 - c],
+            v.part_in.at[tower],
+            v.part_sem.at[0, tower, 0],
+            v.part_sem.at[1, tower, 0],
+            sibling,
+        )
+    for tower in (first, second):
+        core_copies[tower].wait_recv()
+        v.last_out[tower] = v.part[tower, c, 1 - high] + v.part_in[tower, 1 - high]
+        last_copies[tower] = send(
+            v.last_out.at[tower],
+            v.last_in.at[tower],
+            v.part_sem.at[0, tower, 1],
+            v.part_sem.at[1, tower, 1],
+            device(z, (x + 2) % 4, y, c),
+        )
     settle(mark)
-    totals = {}
     for tower in (first, second):
-        total = v.part[tower, d % 4]
-        for k in (1, 2, 3):
-            part_copies[tower][3 - k].wait_recv()
-            total += v.part_in[tower, k]
-        totals[tower] = total[:, :192]
+        total = v.part[tower, c, high] + v.part_in[tower, high]
+        last_copies[tower].wait_recv()
+        totals[tower] = (total + v.last_in[tower])[:, :192]
     output[...] = jnp.concatenate([totals[0], totals[1]], axis=1)
     settle(len(sends))
 

time: 104 us -> 104 us (level)
  no operation moved by 1% of the time
where the time goes in v4:
time: 104 us
  Pallas kernels  101 us (97%)
  between operations  1.93 us (2%)
  local copies, waits for them, and re-layouts  1.58 us (2%)
    pallas_call x1, Pallas kernels, on_device(): pl.pallas_call(window_kernel, out_shape=jax.ShapeDtypeStruct((48, 384), F...  101 us

profile of v4, /device:TPU:1, one launch (start us, length us, event | category | flops | bytes accessed | tf_op | source)
XLA Modules:
  0.0 104.2 jit_solution(10052480538777984445)
XLA Ops:
  1.9 100.7 %shard_map.113 = f32[48,384]{1,0:T(8,128)} custom-call(bf16[256,768]{1,0:T(8,128)(2,1)} %refs_0_.1, bf16[768,1536]{1,0:T(8,128)(2,1)} %refs_1_.1, bf16[192,1536]{1,0:T(8,128)(2,1)} %refs_2_.1, bf16[192,256]{1,0:T(8,128)(2,1)} %bitcast.6, bf16[256,768]{1,0:T(8,128)(2,1)} %refs_4_.1, bf16[768,1536]{1,0:T(8,128)(2,1)} %refs_5_.1, bf16[192,1536]{1,0:T(8,128)(2,1)} %refs_6_.1, ...), custom_call_target="tpu_custom_call" | custom-call | tf_op jit(solution)/shard_map/pallas_call | solution.py:669
  102.6 1.6 %slice_bitcast_fusion = (f32[192,48]{0,1:T(8,128)}, f32[192,48]{0,1:T(8,128)}) fusion(f32[48,384]{1,0:T(8,128)} %shard_map.113), kind=kLoop, calls=%fused_computation | loop fusion | bytes 147456 | tf_op jit(solution)/shard_map/transpose | solution.py:691
